TPU v7x, 32 devices: a whole 2x2x4 slice. The times are simulated.
32 devices in a mesh: groups: 2 (over y), tile: 4 (over z), chan: 2 (over x), sub: 2 (over core).
Axes of the slice: x: 2, y: 2, z: 4, core: 2. Of those that a mesh axis runs over, the one named last changes fastest.
Arguments:
- residual: float32 [8, 8, 64, 128], P(('groups', 'tile'), None, 'sub'), parts along dimension 0, may hold values from -6 to 6
- coefficients: bfloat16 [8, 8, 128, 64, 128], P(('groups', 'tile'), None, 'chan', 'sub'), parts along dimension 0, may hold values from -6 to 6
- filter_store: float32 [16, 128, 2048], P(('groups', 'tile'), 'chan'), parts along dimension 0, may hold values from -6.4 to 6.4
- plan: int32 [2], replicated, may hold values from 0 to 7
- owner: int32 [8], replicated, may hold values from 0 to 7, as said below
Outputs:
- residual_out: float32 [8, 8, 64, 128], P(('groups', 'tile'), None, 'sub'), parts along dimension 0
- new_coefficients: bfloat16 [8, 2, 128, 64, 128], P(('groups', 'tile'), None, 'chan', 'sub'), parts along dimension 0
- store_out: float32 [16, 128, 2048], P(('groups', 'tile'), 'chan'), parts along dimension 0
There are 2 independent parts, one for each index of `groups`. A program takes and returns all parts, laid end to end along the dimension named above; an argument that names none is the same for every part. Nothing has to cross between parts.
Inputs may be any that keep to these rules, and one draw needn't show every extreme that they name: `owner`: distinct slots, one for each of the 8 blocks; slot s lies on tile device s // 2 at position s % 2.
All inputs are finite; a program needn't handle non-finite values.
Results may differ from a plain program's by a relative error of at most 0.017.
Values may be sent and summed in bfloat16 or wider, within the bound.
A program may use at most 128 MiB of HBM per device.

v0:
```python
import jax
import jax.numpy as jnp
from jax import lax
from jax.sharding import PartitionSpec as P

C = 8
PATCH = 16
STEPS = 2
ROWS = 32
COLS = 128
FEAT = 2048


COEFF_STEP = 0.5
THRESHOLD = 0.3
FILTER_STEP = 40.0


def broadcast(x, axis, root):
    mine = lax.axis_index(axis) == root
    return lax.psum(jnp.where(mine, x, jnp.zeros_like(x)), axis)


def extended(x, sides, width):
    for axis, dim in sides:
        count, length = (lax.axis_size(axis), x.shape[dim])
        up = [(i, (i + 1) % count) for i in range(count - 1)]
        down = [(j, i) for i, j in up]
        last = lax.slice_in_dim(x, length - width, length, axis=dim)
        leading = lax.slice_in_dim(x, 0, width, axis=dim)
        before = lax.ppermute(last, axis, up)
        after = lax.ppermute(leading, axis, down)
        x = jnp.concatenate([before, x, after], axis=dim)
    return x


def correlate(inputs, weights, column_pads):
    return lax.conv_general_dilated(
        inputs[None],
        weights,
        (1, 1),
        ((0, 0), column_pads),
        dimension_numbers=("NCHW", "OIHW", "NCHW"),
        preferred_element_type=jnp.float32,
    )[0]


def shrink(values):
    return jnp.sign(values) * jnp.maximum(jnp.abs(values) - THRESHOLD, 0.0)


def filter_gradient(fresh_wide, target):
    local_count = fresh_wide.shape[0]
    row_count = target.shape[1]
    col_count = target.shape[2]
    widened = jnp.pad(fresh_wide, ((0, 0), (0, 0), (8, 7)))

    def one_row(offset, totals):
        band = lax.dynamic_slice_in_dim(widened, offset, row_count, 1)
        shifts = jnp.stack([band[:, :, column : column + col_count] for column in range(PATCH)])
        piece = jnp.einsum("qkij,cij->kcq", shifts, target, preferred_element_type=jnp.float32)
        return lax.dynamic_update_slice(totals, piece[:, :, None, :], (0, 0, offset, 0))

    empty = jnp.zeros((local_count, C, PATCH, PATCH), jnp.float32)
    return lax.fori_loop(0, PATCH, one_row, empty)


def per_device(residual, coefficients, filter_store, plan, owner):
    scaling = FEAT ** (-0.5)
    sub_count = lax.axis_size("sub")
    tile_place = lax.axis_index("tile")
    pixel_total = float(lax.axis_size("tile") * sub_count * ROWS * COLS)
    current = residual[0]
    coeffs = coefficients
    store = filter_store
    slot_count = store.shape[0]
    local_count = store.shape[1]
    updated = []
    for step_index in range(STEPS):
        block = plan[step_index]
        holder = owner[block]
        sender = holder // slot_count
        position = holder % slot_count
        master = lax.dynamic_index_in_dim(store, position, 0, keepdims=False)
        shared = broadcast(master.astype(jnp.bfloat16), "tile", sender)
        kernel = shared.reshape(local_count, C, PATCH, PATCH)
        flipped = kernel[:, :, ::-1, ::-1]
        previous = lax.dynamic_index_in_dim(coeffs[0], block, 0, keepdims=False)
        rounded = current.astype(jnp.bfloat16)
        padded = extended(rounded, (("sub", 1),), 8)
        adjoint = scaling * correlate(padded[:, 1:], flipped, (7, 8))
        previous_wide = previous.astype(jnp.float32)
        fresh = shrink(previous_wide - COEFF_STEP * adjoint).astype(jnp.bfloat16)
        change = (fresh.astype(jnp.float32) - previous_wide).astype(jnp.bfloat16)
        stacked = extended(jnp.stack([change, fresh]), (("sub", 2),), 8)
        change_wide = stacked[0]
        fresh_wide = stacked[1]
        partial_sum = correlate(change_wide[:, : ROWS + 15], kernel.transpose(1, 0, 2, 3), (8, 7))
        total = lax.psum(partial_sum.astype(jnp.bfloat16), "chan").astype(jnp.float32)
        current = current + scaling * total
        target = current.astype(jnp.bfloat16)
        local_grads = filter_gradient(fresh_wide, target)
        grads = lax.psum(local_grads.reshape(local_count, FEAT), ("tile", "sub"))
        moved = master - FILTER_STEP * grads / pixel_total
        length = jnp.sqrt(jnp.sum(moved * moved, axis=1, keepdims=True)) * scaling
        final = moved / jnp.maximum(length, 1.0)
        written = lax.dynamic_update_index_in_dim(store, final, position, 0)
        store = jnp.where(tile_place == sender, written, store)
        coeffs = lax.dynamic_update_index_in_dim(coeffs, fresh[None], block, 1)
        updated.append(fresh)
    return (current[None], jnp.stack(updated, axis=0)[None], store)


def solution(mesh):
    placed = (
        P(("groups", "tile"), None, "sub", None),
        P(("groups", "tile"), None, "chan", "sub", None),
        P(("groups", "tile"), "chan", None),
        P(),
        P(),
    )
    return jax.shard_map(
        per_device,
        mesh=mesh,
        in_specs=placed,
        out_specs=(
            P(("groups", "tile"), None, "sub", None),
            P(("groups", "tile"), None, "chan", "sub", None),
            P(("groups", "tile"), "chan", None),
        ),
        check_vma=False,
    )
```

profile of v0, /device:TPU:0, one launch (start us, length us, event | category | flops | bytes accessed | tf_op | source)
XLA Modules:
  0.0 1433.1 jit_solution(8234015209350277915)
XLA Ops:
  16.4 1.8 copy.113
  22.2 3.8 collective-permute-start
  25.9 15.6 %copy.109 = bf16[1,8,64,32,128]{2,3,4,1,0:T(8,128)(2,1)} copy(bf16[1,8,64,32,128]{4,3,2,1,0:T(8,128)(2,1)} %param.10) | data formatting | bytes 8388608 | tf_op args[1]
  44.7 16.1 %all-reduce.9.cloned.1.call-done = bf16[64,8,16,16]{0,1,3,2:T(8,128)(2,1)} async-done(((bf16[64,8,16,16]{0,1,3,2:T(8,128)(2,1)}), bf16[64,8,16,16]{0,1,3,2:T(8,128)(2,1)}) %all-reduce.9.cloned.1.call-update) | async-done | bytes 262160 | tf_op jit(solution)/shard_map/psum | solution.py:21
  60.8 8.3 select_multiply_fusion.1
  70.0 3.1 fusion.70
  74.6 3.3 collective-permute-start.2
  83.0 167.1 %fusion.48 = bf16[32,8,18,8]{3,1,2,0:T(8,128)(2,1)S(1)} fusion(bf16[64,8,16,16]{0,1,3,2:T(8,128)(2,1)S(1)} %copy-done.17, bf16[64,47,8,33]{0,2,3,1:T(8,128)(2,1)S(1)} %fusion.116), kind=kOutput, calls=%fused_computation.84 | convolution fusion | flops 1207959552 | bytes 1924096 | tf_op jit(solution)/shard_map/conv_general_dilated | solution.py:38
  253.7 21.7 %all-reduce.11.cloned.1.call-done = bf16[8,32,128]{1,0,2:T(8,128)(2,1)} async-done(((bf16[8,32,128]{1,0,2:T(8,128)(2,1)}), bf16[8,32,128]{1,0,2:T(8,128)(2,1)}) %all-reduce.11.cloned.1.call-update) | async-done | bytes 65552 | tf_op jit(solution)/shard_map/psum | solution.py:99
  276.8 377.9 %while.26 = (s32[]{:T(128)}, f32[64,8,16,16]{0,3,2,1:T(8,128)S(1)}, bf16[64,48,143]{2,0,1:T(8,128)(2,1)S(1)}, bf16[8,32,128]{2,0,1:T(8,128)(2,1)S(1)}, s32[]{:T(...) while((s32[]{:T(128)}, f32[64,8,16,16]{0,3,2,1:T(8,128)S(1)}, ...), condition=%wide.region_3.4_spmd, body=%wide.region_2.3_spmd.sunk | while | flops 67108880 | bytes 25395704 | solution.py:65
  293.7 6.7 convolution_bitcast_fusion.4
  317.3 6.7 convolution_bitcast_fusion.4
  340.9 6.7 convolution_bitcast_fusion.4
  364.5 6.7 convolution_bitcast_fusion.4
  388.1 6.7 convolution_bitcast_fusion.4
  411.8 6.7 convolution_bitcast_fusion.4
  435.4 6.7 convolution_bitcast_fusion.4
  459.0 6.7 convolution_bitcast_fusion.4
  482.6 6.7 convolution_bitcast_fusion.4
  506.2 6.7 convolution_bitcast_fusion.4
  529.9 6.7 convolution_bitcast_fusion.4
  553.5 6.7 convolution_bitcast_fusion.4
  577.1 6.7 convolution_bitcast_fusion.4
  600.7 6.7 convolution_bitcast_fusion.4
  624.3 6.7 convolution_bitcast_fusion.4
  648.0 6.7 convolution_bitcast_fusion.4
  655.7 10.1 all-reduce.15.cloned.1.call-start
  669.7 8.3 copy.196
  680.2 4.4 collective-permute-start.4
  684.6 30.0 %all-reduce.13.cloned.1.call-done = f32[64,2048]{0,1:T(8,128)} async-done(((f32[64,2048]{0,1:T(8,128)}), f32[64,2048]{0,1:T(8,128)}) %all-reduce.13.cloned.1.call-update) | async-done | bytes 524304 | tf_op jit(solution)/shard_map/psum | solution.py:103
  714.6 1.5 multiply_reduce_fusion.1
  717.6 1.4 copy.126
  719.1 3.8 fusion.80
  726.1 30.3 %all-reduce.15.cloned.1.call-done = bf16[64,8,16,16]{0,1,3,2:T(8,128)(2,1)} async-done(((bf16[64,8,16,16]{0,1,3,2:T(8,128)(2,1)}), bf16[64,8,16,16]{0,1,3,2:T(8,128)(2,1)}) %all-reduce.15.cloned.1.call-update) | async-done | bytes 262160 | tf_op jit(solution)/shard_map/psum | solution.py:21
  756.5 8.4 select_multiply_fusion
  765.6 2.3 fusion.69
  769.4 3.3 collective-permute-start.6
  777.9 167.4 %fusion.52 = bf16[32,8,18,8]{3,1,2,0:T(8,128)(2,1)S(1)} fusion(bf16[64,8,16,16]{0,1,3,2:T(8,128)(2,1)S(1)} %copy-done.18, bf16[64,47,8,33]{0,2,3,1:T(8,128)(2,1)S(1)} %fusion.118), kind=kOutput, calls=%fused_computation.87 | convolution fusion | flops 1207959552 | bytes 1924096 | tf_op jit(solution)/shard_map/conv_general_dilated | solution.py:38
  948.8 21.7 %all-reduce.17.cloned.1.call-done = bf16[8,32,128]{1,0,2:T(8,128)(2,1)} async-done(((bf16[8,32,128]{1,0,2:T(8,128)(2,1)}), bf16[8,32,128]{1,0,2:T(8,128)(2,1)}) %all-reduce.17.cloned.1.call-update) | async-done | bytes 65552 | tf_op jit(solution)/shard_map/psum | solution.py:99
  970.6 1.8 fusion.86
  973.7 388.7 %while.27 = (s32[]{:T(128)}, f32[64,8,16,16]{0,3,2,1:T(8,128)}, bf16[64,48,143]{2,0,1:T(8,128)(2,1)S(1)}, bf16[8,32,128]{2,0,1:T(8,128)(2,1)S(1)}, s32[]{:T(128)...) while((s32[]{:T(128)}, f32[64,8,16,16]{0,3,2,1:T(8,128)}, ...), condition=%wide.region_9.10_spmd, body=%wide.region_8.9_spmd.sunk | while | flops 67108880 | bytes 25362936 | solution.py:65
  990.6 6.7 convolution_bitcast_fusion.5
  1014.9 6.7 convolution_bitcast_fusion.5
  1039.2 6.7 convolution_bitcast_fusion.5
  1063.5 6.7 convolution_bitcast_fusion.5
  1087.8 6.7 convolution_bitcast_fusion.5
  1112.1 6.7 convolution_bitcast_fusion.5
  1136.4 6.7 convolution_bitcast_fusion.5
  1160.7 6.7 convolution_bitcast_fusion.5
  1185.0 6.7 convolution_bitcast_fusion.5
  1209.3 6.7 convolution_bitcast_fusion.5
  1233.6 6.7 convolution_bitcast_fusion.5
  1257.9 6.7 convolution_bitcast_fusion.5
  1282.1 6.7 convolution_bitcast_fusion.5
  1306.4 6.7 convolution_bitcast_fusion.5
  1330.7 6.7 convolution_bitcast_fusion.5
  1355.0 6.7 convolution_bitcast_fusion.5
  1362.4 2.4 constant_dynamic-slice_fusion
  1364.8 3.2 fusion.68
  1368.0 5.3 copy.135
  1373.2 1.9 copy.134
  1375.1 46.3 %all-reduce.19.cloned.1.call-done = f32[64,2048]{0,1:T(8,128)} async-done(((f32[64,2048]{0,1:T(8,128)}), f32[64,2048]{0,1:T(8,128)}) %all-reduce.19.cloned.1.call-update) | async-done | bytes 524304 | tf_op jit(solution)/shard_map/psum | solution.py:103
  1421.4 1.5 multiply_reduce_fusion
  1424.3 1.6 copy.136
  (664 shorter events, 595.7 us)
Async XLA Ops:
  7.2 12.6 copy-start.14
  7.2 53.7 %all-reduce.9.cloned.1.call-start = ((), (), s32[]{:S(2)}) async-start(), calls=%async_computation | async-start | bytes 1048576 | tf_op jit(solution)/shard_map/psum | solution.py:21
  18.2 23.4 %copy-start = (f32[2,64,2048]{1,2,0:T(8,128)}, f32[2,64,2048]{1,2,0:T(8,128)S(1)}, u32[]{:S(2)}) copy-start(f32[2,64,2048]{1,2,0:T(8,128)S(1)} %copy.113) | copy-start | bytes 3145732
  19.7 255.8 %all-reduce.11.cloned.1.call-start = ((), (), s32[]{:S(2)}) async-start(), calls=%async_computation.1 | async-start | bytes 524288 | tf_op jit(solution)/shard_map/psum | solution.py:99
  20.0 21.6 %copy-start.8 = (f32[1,8,32,128]{2,1,3,0:T(8,128)}, f32[1,8,32,128]{2,1,3,0:T(8,128)S(1)}, u32[]{:S(2)}) copy-start(f32[1,8,32,128]{2,1,3,0:T(8,128)S(1)} %copy.108) | copy-start | bytes 393220
  20.9 20.7 %collective-permute-start.1 = (bf16[8,8,128]{1,0,2:T(8,128)(2,1)}, bf16[8,8,128]{1,0,2:T(8,128)(2,1)S(1)}, u32[]{:S(2)}, u32[]{:S(2)}) collective-permute-start(bf16[8,8,128]{1,0,2:T(8,128)(2,1)} %get-tuple-element.248), channel_id=1, source_target_pairs={{1,0},{3,2},{5,4},{7,6},{9,8},{11,10},{13,12},{15,14},{17,16},{19,... | collective-permute-start | bytes 49160 | tf_op jit(solution)/shard_map/ppermute | solution.py:32
  22.2 19.4 %collective-permute-start = (bf16[8,8,128]{1,0,2:T(8,128)(2,1)S(1)}, bf16[8,8,128]{1,0,2:T(8,128)(2,1)}, u32[]{:S(2)}, u32[]{:S(2)}) collective-permute-start(bf16[8,8,128]{1,0,2:T(8,128)(2,1)S(1)} %get-tuple-element.247), channel_id=1, source_target_pairs={{0,1},{2,3},{4,5},{6,7},{8,9},{10,11},{12,13},{14,15},{16,17},{18,... | collective-permute-start | bytes 49160 | tf_op jit(solution)/shard_map/ppermute | solution.py:31
  41.6 19.3 %copy-start.19 = (pred[8,18]{0,1:T(8,128)(4,1)S(1)}, pred[8,18]{0,1:T(8,128)(4,1)}, u32[]{:S(2)}) copy-start(pred[8,18]{0,1:T(8,128)(4,1)} %constant.176) | copy-start | bytes 436
  70.0 3.3 copy-start.4
  73.1 6.1 copy-start.5
  73.3 4.7 collective-permute-start.3
  74.6 4.6 collective-permute-start.2
  82.0 1.0 copy-start.17
  83.0 168.1 %copy-start.15 = (pred[8,18]{1,0:T(8,128)(4,1)S(1)}, pred[8,18]{1,0:T(8,128)(4,1)}, u32[]{:S(2)}) copy-start(pred[8,18]{1,0:T(8,128)(4,1)} %constant.172) | copy-start | bytes 436
  251.1 24.3 %copy-start.9 = (f32[1,8,32,128]{2,1,3,0:T(8,128)S(1)}, f32[1,8,32,128]{2,1,3,0:T(8,128)}, u32[]{:S(2)}) copy-start(f32[1,8,32,128]{2,1,3,0:T(8,128)} %copy-done.8) | copy-start | bytes 393220
  252.1 462.5 %all-reduce.13.cloned.1.call-start = ((), (), s32[]{:S(2)}) async-start(), calls=%async_computation.2 | async-start | bytes 2097152 | tf_op jit(solution)/shard_map/psum | solution.py:103
  654.7 1.0 copy-start.12
  655.7 100.8 %all-reduce.15.cloned.1.call-start = ((), (), s32[]{:S(2)}) async-start(), calls=%async_computation.3 | async-start | bytes 1048576 | tf_op jit(solution)/shard_map/psum | solution.py:21
  669.7 44.9 %copy-start.1 = (f32[2,64,2048]{1,2,0:T(8,128)S(1)}, f32[2,64,2048]{1,2,0:T(8,128)}, u32[]{:S(2)}) copy-start(f32[2,64,2048]{1,2,0:T(8,128)} %copy-done) | copy-start | bytes 3145732
  678.9 44.0 %collective-permute-start.5 = (bf16[8,8,128]{1,0,2:T(8,128)(2,1)}, bf16[8,8,128]{1,0,2:T(8,128)(2,1)}, u32[]{:S(2)}, u32[]{:S(2)}) collective-permute-start(bf16[8,8,128]{1,0,2:T(8,128)(2,1)} %get-tuple-element.246), channel_id=1, source_target_pairs={{1,0},{3,2},{5,4},{7,6},{9,8},{11,10},{13,12},{15,14},{17,16},{19,... | collective-permute-start | bytes 49160 | tf_op jit(solution)/shard_map/ppermute | solution.py:32
  680.2 42.8 %collective-permute-start.4 = (bf16[8,8,128]{1,0,2:T(8,128)(2,1)}, bf16[8,8,128]{1,0,2:T(8,128)(2,1)}, u32[]{:S(2)}, u32[]{:S(2)}) collective-permute-start(bf16[8,8,128]{1,0,2:T(8,128)(2,1)} %get-tuple-element.245), channel_id=1, source_target_pairs={{0,1},{2,3},{4,5},{6,7},{8,9},{10,11},{12,13},{14,15},{16,17},{18,... | collective-permute-start | bytes 49160 | tf_op jit(solution)/shard_map/ppermute | solution.py:31
  717.6 5.4 copy-start.2
  719.1 251.5 %all-reduce.17.cloned.1.call-start = ((), (), s32[]{:S(2)}) async-start(), calls=%async_computation.4 | async-start | bytes 524288 | tf_op jit(solution)/shard_map/psum | solution.py:99
  722.9 33.5 %copy-start.20 = (pred[8,18]{0,1:T(8,128)(4,1)S(1)}, pred[8,18]{0,1:T(8,128)(4,1)}, u32[]{:S(2)}) copy-start(pred[8,18]{0,1:T(8,128)(4,1)} %constant.176) | copy-start | bytes 436
  767.9 6.1 copy-start.7
  768.1 4.6 collective-permute-start.7
  769.4 4.6 collective-permute-start.6
  776.8 1.0 copy-start.18
  777.9 168.4 %copy-start.16 = (pred[8,18]{1,0:T(8,128)(4,1)S(1)}, pred[8,18]{1,0:T(8,128)(4,1)}, u32[]{:S(2)}) copy-start(pred[8,18]{1,0:T(8,128)(4,1)} %constant.172) | copy-start | bytes 436
  946.2 24.3 %copy-start.10 = (f32[1,8,32,128]{2,1,3,0:T(8,128)S(1)}, f32[1,8,32,128]{2,1,3,0:T(8,128)}, u32[]{:S(2)}) copy-start(f32[1,8,32,128]{2,1,3,0:T(8,128)} %copy-done.8) | copy-start | bytes 393220
  946.2 24.3 %copy-start.13 = (bf16[8,32,128]{1,0,2:T(8,128)(2,1)S(1)}, bf16[8,32,128]{1,0,2:T(8,128)(2,1)}, u32[]{:S(2)}) copy-start(bf16[8,32,128]{1,0,2:T(8,128)(2,1)} %all-reduce.11.cloned.1.call-done) | copy-start | bytes 196612
  947.2 474.2 %all-reduce.19.cloned.1.call-start = ((), (), s32[]{:S(2)}) async-start(), calls=%async_computation.5 | async-start | bytes 2097152 | tf_op jit(solution)/shard_map/psum | solution.py:103
  1362.4 2.4 copy-start.6
  1364.8 56.6 %copy-start.3 = (f32[2,64,2048]{1,2,0:T(8,128)S(1)}, f32[2,64,2048]{1,2,0:T(8,128)}, u32[]{:S(2)}) copy-start(f32[2,64,2048]{1,2,0:T(8,128)} %copy-done.2) | copy-start | bytes 3145732
  1368.0 55.0 %copy-start.11 = (f32[1,64,2048]{1,2,0:T(8,128)S(1)}, f32[1,64,2048]{1,2,0:T(8,128)}, u32[]{:S(2)}) copy-start(f32[1,64,2048]{1,2,0:T(8,128)} %constant_dynamic-slice_fusion) | copy-start | bytes 1572868
Sparse Core Ops, SparseCore 0:
  19.8 40.9 all-reduce.8
  252.2 23.1 all-reduce.10
  655.8 58.7 all-reduce.12
  719.2 37.2 all-reduce.14
  947.3 23.1 all-reduce.16
  1362.5 58.8 all-reduce.18
where the time goes:
time: 1440 us; the launch traced here: 1430 us
  local copies, waits for them, and re-layouts  616 us (43%)
  matrix products  566 us (39%)
  waiting for transfers between devices  169 us (12%)
  starting transfers between devices  30.3 us (2%)
  other arithmetic  27.5 us (2%)
  between operations  24.2 us (2%)
    while x480, local copies, waits for them, and re-layouts  505 us
    conv_general_dilated x4, matrix products, correlate(): lax.conv_general_dilated(inputs[None], weights, (1, 1), ((0, 0), column_p...  351 us
    dot_general x32, matrix products, one_row(): jnp.einsum('qkij,cij->kcq', shifts, target, preferred_element_type=jnp.fl...  215 us
    psum x2, waiting for transfers between devices, per_device(): grads = lax.psum(local_grads.reshape(local_count, FEAT), ('tile', 'sub'))  76.3 us
    psum x2, waiting for transfers between devices, broadcast(): return lax.psum(jnp.where(mine, x, jnp.zeros_like(x)), axis)  46.4 us
    psum x2, waiting for transfers between devices, per_device(): lax.psum(partial_sum.astype(jnp.bfloat16), 'chan').astype(jnp.float32)  43.5 us
    unnamed x51, local copies, waits for them, and re-layouts  38.4 us
    another operation x32, local copies, waits for them, and re-layouts, one_row(): jnp.stack([band[:, :, column:column + col_count] for column in range(PATC...  34.7 us
  transfers between devices with their start and end apart: 14, of which 8 were waited for; matrix products, arithmetic and copies ran while one was open for 4% of the time, Pallas kernels for 0%

commit v1 on v0

v1 whole, which is shorter than its diff:
```python
import functools

import jax
import jax.numpy as jnp
from jax import lax
from jax.experimental import pallas as pl
from jax.experimental.pallas import tpu as pltpu
from jax.sharding import PartitionSpec as P

C = 8
PATCH = 16
STEPS = 2
ROWS = 32
COLS = 128
FEAT = 2048
HALO = 8
PADDED = ROWS + 2 * HALO
HALF = ROWS // 2
QC = PATCH * C

COEFF_STEP = 0.5
THRESHOLD = 0.3
FILTER_STEP = 40.0

BF16 = jnp.bfloat16
F32 = jnp.float32
VMEM_LIMIT = 40 * 1024 * 1024


def call(body, out_shape, scratch, flops, args):
    return pl.pallas_call(
        body,
        out_shape=out_shape,
        in_specs=[pl.BlockSpec(memory_space=pltpu.VMEM)] * len(args),
        out_specs=jax.tree.map(lambda _: pl.BlockSpec(memory_space=pltpu.VMEM), out_shape),
        scratch_shapes=scratch,
        compiler_params=pltpu.CompilerParams(vmem_limit_bytes=VMEM_LIMIT),
        cost_estimate=pl.CostEstimate(flops=flops, bytes_accessed=2 << 20, transcendentals=0),
    )(*args)


def shifted_rows(x, lanes):
    pieces = []
    for q in range(PATCH):
        moved = pltpu.roll(x, (q - HALO) % COLS, 1) if q != HALO else x
        source = lanes - (q - HALO)
        pieces.append(jnp.where((source >= 0) & (source < COLS), moved, 0.0))
    return jnp.concatenate(pieces, axis=0).astype(BF16)


def adjoint_body(count, x_ref, w_ref, prev_ref, fresh_ref, change_ref, xq):
    lanes = lax.broadcasted_iota(jnp.int32, (C, COLS), 1)

    def spread(r, carry):
        xq[pl.ds(pl.multiple_of(r * QC, QC), QC), :] = shifted_rows(x_ref[r], lanes)
        return carry

    lax.fori_loop(0, PADDED, spread, 0)
    depth = PATCH * QC

    def row_pair(i, carry):
        upper = xq[pl.ds(pl.multiple_of((i + 1) * QC, QC), depth), :]
        lower = xq[pl.ds(pl.multiple_of((i + 1 + HALF) * QC, QC), depth), :]
        both = jnp.concatenate([upper, lower], axis=1)
        sums = jnp.dot(w_ref[...], both, preferred_element_type=F32)
        for at in range(2):
            row = i + at * HALF
            before = prev_ref[row].astype(F32)
            adjoint = FEAT ** (-0.5) * sums[:, at * COLS : (at + 1) * COLS]
            v = before - COEFF_STEP * adjoint
            soft = jnp.where(v > THRESHOLD, v - THRESHOLD, jnp.where(v < -THRESHOLD, v + THRESHOLD, 0.0))
            fresh = soft.astype(BF16)
            fresh_ref[row] = fresh
            change_ref[row] = (fresh.astype(F32) - before).astype(BF16)
        return carry

    lax.fori_loop(0, HALF, row_pair, 0)


def fill(padded, before_ref, main_ref, after_ref, count):
    edge = HALO * count
    padded[0:edge, :] = before_ref[...]
    padded[edge : edge + ROWS * count, :] = main_ref[...]
    padded[edge + ROWS * count : 2 * edge + ROWS * count, :] = after_ref[...]


def synthesis_body(count, w_ref, before_ref, main_ref, after_ref, out_ref, padded, v_ref):
    lanes = lax.broadcasted_iota(jnp.int32, (C, COLS), 1)
    fill(padded, before_ref, main_ref, after_ref, count)
    group = COLS // count
    for base in range(0, PATCH, group):
        blocks = []
        for p in range(base, base + group):
            m = PATCH - 1 - p
            blocks.append(w_ref[:, m * QC : (m + 1) * QC].astype(F32))
        stacked = jnp.concatenate(blocks, axis=0)
        v_ref[:, base * count : (base + group) * count] = stacked.T.astype(BF16)
    depth = PATCH * count

    def row_pair(i, carry):
        upper = padded[pl.ds(pl.multiple_of(i * count, count), depth), :]
        lower = padded[pl.ds(pl.multiple_of((i + HALF) * count, count), depth), :]
        both = jnp.concatenate([upper, lower], axis=1)
        z = jnp.dot(v_ref[...], both, preferred_element_type=F32)
        for at in range(2):
            total = jnp.zeros((C, COLS), F32)
            for q in range(PATCH):
                part = z[q * C : (q + 1) * C, at * COLS : (at + 1) * COLS]
                moved = pltpu.roll(part, (HALO - q) % COLS, 1) if q != HALO else part
                source = lanes + (q - HALO)
                total = total + jnp.where((source >= 0) & (source < COLS), moved, 0.0)
            out_ref[i + at * HALF] = total.astype(BF16)
        return carry

    lax.fori_loop(0, HALF, row_pair, 0)


def gradient_body(count, x_ref, before_ref, main_ref, after_ref, out_ref, padded, total):
    lanes = lax.broadcasted_iota(jnp.int32, (C, COLS), 1)
    fill(padded, before_ref, main_ref, after_ref, count)
    total[...] = jnp.zeros_like(total)
    depth = PATCH * count

    def row_pair(i, carry):
        upper = padded[pl.ds(pl.multiple_of(i * count, count), depth), :]
        lower = padded[pl.ds(pl.multiple_of((i + HALF) * count, count), depth), :]
        both = jnp.concatenate([upper, lower], axis=1)
        target = jnp.concatenate([shifted_rows(x_ref[i], lanes), shifted_rows(x_ref[i + HALF], lanes)], axis=1)
        total[...] += lax.dot_general(both, target, (((1,), (1,)), ((), ())), preferred_element_type=F32)
        return carry

    lax.fori_loop(0, HALF, row_pair, 0)
    for p in range(PATCH):
        out_ref[:, p * QC : (p + 1) * QC] = total[p * count : (p + 1) * count, :]


def swap_halo(x, place):
    send = jnp.where(place == 0, x[ROWS - HALO :], x[:HALO])
    got = lax.ppermute(send, "sub", [(0, 1), (1, 0)])
    empty = jnp.zeros_like(got)
    return jnp.where(place == 1, got, empty), jnp.where(place == 0, got, empty)


def per_device(residual, coefficients, filter_store, plan, owner):
    scaling = FEAT ** (-0.5)
    sub_place = lax.axis_index("sub")
    tile_place = lax.axis_index("tile")
    pixel_total = float(lax.axis_size("tile") * lax.axis_size("sub") * ROWS * COLS)
    slot_count, count = filter_store.shape[:2]
    holders = [owner[plan[s]] for s in range(STEPS)]
    macs = 2 * count * FEAT * ROWS * COLS

    def picked(store, s):
        return lax.dynamic_index_in_dim(store, holders[s] % slot_count, 0, keepdims=False)

    def shared(stores):
        sent = [
            jnp.where(tile_place == holders[s] // slot_count, picked(store, s).astype(BF16), jnp.zeros((), BF16))
            for s, store in stores
        ]
        whole = lax.psum(jnp.stack(sent), "tile")
        cut = whole.reshape(-1, count, C, PATCH, PATCH)[:, :, :, ::-1]
        return cut.transpose(0, 1, 3, 4, 2).reshape(-1, count, FEAT)

    def updated(store, s, grads):
        master = picked(store, s)
        moved = master - FILTER_STEP * grads / pixel_total
        length = jnp.sqrt(jnp.sum(moved * moved, axis=1, keepdims=True)) * scaling
        final = moved / jnp.maximum(length, 1.0)
        written = lax.dynamic_update_index_in_dim(store, final, holders[s] % slot_count, 0)
        return jnp.where(tile_place == holders[s] // slot_count, written, store)

    def summed(local):
        whole = lax.psum(local, ("tile", "sub"))
        return whole.reshape(count, PATCH, PATCH, C).transpose(0, 3, 1, 2).reshape(count, FEAT)

    current = residual[0].transpose(1, 0, 2)
    first_pair = shared([(0, filter_store), (1, filter_store)])
    weights = first_pair[0]
    fresh_maps, local_grads, sums = [], [], []
    same = plan[0] == plan[1]
    for s in range(STEPS):
        previous = lax.dynamic_index_in_dim(coefficients[0], plan[s], 0, keepdims=False).transpose(1, 0, 2)
        if s == 1:
            previous = jnp.where(same, fresh_maps[0], previous)
            weights = lax.cond(
                same,
                lambda local, pair: shared([(1, updated(filter_store, 0, summed(local)))])[0],
                lambda local, pair: pair[1],
                local_grads[0],
                first_pair,
            )
        rounded = current.astype(BF16)
        before, after = swap_halo(rounded, sub_place)
        padded = jnp.concatenate([before, rounded, after], axis=0).astype(F32)
        maps = jax.ShapeDtypeStruct((ROWS, count, COLS), BF16)
        fresh, change = call(
            functools.partial(adjoint_body, count),
            (maps, maps),
            [pltpu.VMEM((PADDED * QC, COLS), BF16)],
            macs,
            (padded, weights, previous),
        )
        edges = swap_halo(jnp.stack([change, fresh], axis=1), sub_place)
        flat = lambda x: x.reshape(-1, COLS)
        space = pltpu.VMEM((PADDED * count, COLS), BF16)
        partial_sum = call(
            functools.partial(synthesis_body, count),
            jax.ShapeDtypeStruct((ROWS, C, COLS), BF16),
            [space, pltpu.VMEM((QC, PATCH * count), BF16)],
            macs,
            (weights, flat(edges[0][:, 0]), flat(change), flat(edges[1][:, 0])),
        )
        if lax.axis_size("chan") == 2:
            other = lax.ppermute(partial_sum, "chan", [(0, 1), (1, 0)])
            total = partial_sum.astype(F32) + other.astype(F32)
        else:
            total = lax.psum(partial_sum, "chan").astype(F32)
        current = current + scaling * total
        target = current.astype(BF16).astype(F32)
        local = call(
            functools.partial(gradient_body, count),
            jax.ShapeDtypeStruct((count, FEAT), F32),
            [space, pltpu.VMEM((PATCH * count, QC), F32)],
            macs,
            (target, flat(edges[0][:, 1]), flat(fresh), flat(edges[1][:, 1])),
        )
        fresh_maps.append(fresh)
        local_grads.append(local)
        sums.append(summed(local))
    store = filter_store
    for s in range(STEPS):
        store = updated(store, s, sums[s])
    coeffs_out = jnp.stack(fresh_maps, axis=0).transpose(0, 2, 1, 3)
    return (current.transpose(1, 0, 2)[None], coeffs_out[None], store)


def solution(mesh):
    placed = (
        P(("groups", "tile"), None, "sub", None),
        P(("groups", "tile"), None, "chan", "sub", None),
        P(("groups", "tile"), "chan", None),
        P(),
        P(),
    )
    return jax.shard_map(
        per_device,
        mesh=mesh,
        in_specs=placed,
        out_specs=(
            P(("groups", "tile"), None, "sub", None),
            P(("groups", "tile"), None, "chan", "sub", None),
            P(("groups", "tile"), "chan", None),
        ),
        check_vma=False,
    )
```

time: 1440 us -> 213 us (0.15)
  local copies, waits for them, and re-layouts: 616 us -> 21.7 us
  matrix products: 566 us -> 0 us
  waiting for transfers between devices: 169 us -> 116 us
  Pallas kernels: 0 us -> 42.4 us
  starting transfers between devices: 30.3 us -> 4.59 us
  other arithmetic: 27.5 us -> 4 us
    while x482 -> x0, local copies, waits for them, and re-layouts: 506 us -> none
    conv_general_dilated x4 -> x0, matrix products: 351 us -> none  [correlate(): lax.conv_general_dilated(inputs[None], weights, (1, 1), ((0, 0), column_p...]
    dot_general x32 -> x0, matrix products: 215 us -> none  [one_row(): jnp.einsum('qkij,cij->kcq', shifts, target, preferred_element_type=jnp.fl...]
    psum x6 -> x2, waiting for transfers between devices: 166 us -> 109 us  [the longest x1 56.1 us: summed(): whole = lax.psum(local, ('tile', 'sub'))]
    pallas_call x0 -> x6, Pallas kernels: none -> 42.4 us  [call(): pl.pallas_call(body, out_shape=out_shape, in_specs=[pl.BlockSpec(memory_s...]
    another operation x34 -> x0, local copies, waits for them, and re-layouts: 35.9 us -> none  [the longest x32 34.7 us: one_row(): jnp.stack([band[:, :, column:column + col_count] for column in range(PATC...]
    unnamed x51 -> x17, local copies, waits for them, and re-layouts: 38.4 us -> 6.73 us
    ppermute x8 -> x6, starting transfers between devices: 20 us -> 4.33 us  [the longest x2 3.08 us: per_device(): other = lax.ppermute(partial_sum, 'chan', [(0, 1), (1, 0)])]
  transfers between devices with their start and end apart: 14 -> 8, of which waited for: 8 -> 6; matrix products, arithmetic and copies ran while one was open for 4% -> 3% of each run, Pallas kernels for 0% -> 3%
where the time goes in v1:
time: 213 us
  waiting for transfers between devices  116 us (54%)
  Pallas kernels  42.4 us (20%)
  between operations  24.3 us (11%)
  local copies, waits for them, and re-layouts  21.7 us (10%)
  starting transfers between devices  4.59 us (2%)
  other arithmetic  4 us (2%)
    psum x1, waiting for transfers between devices, summed(): whole = lax.psum(local, ('tile', 'sub'))  56.1 us
    psum x1, waiting for transfers between devices, shared(): whole = lax.psum(jnp.stack(sent), 'tile')  52.5 us
    pallas_call x6, Pallas kernels, call(): pl.pallas_call(body, out_shape=out_shape, in_specs=[pl.BlockSpec(memory_s...  42.4 us
    unnamed x17, local copies, waits for them, and re-layouts  6.73 us
    div x4, local copies, waits for them, and re-layouts, updated(): moved = master - FILTER_STEP * grads / pixel_total  6.57 us
    ppermute x2, waiting for transfers between devices, per_device(): other = lax.ppermute(partial_sum, 'chan', [(0, 1), (1, 0)])  5.52 us
  transfers between devices with their start and end apart: 8, of which 6 were waited for; matrix products, arithmetic and copies ran while one was open for 3% of the time, Pallas kernels for 3%

profile of v1, /device:TPU:0, one launch (start us, length us, event | category | flops | bytes accessed | tf_op | source)
XLA Modules:
  0.0 212.6 jit_solution(743440674799203860)
XLA Ops:
  7.2 0.0 all-reduce.10.cloned.1.call-start
  7.2 1.3 fusion.20
  12.4 1.3 fusion.19
  18.5 1.8 copy.22
  20.3 0.0 copy-start
  20.4 0.1 fusion.7
  20.5 0.2 pad_maximum_fusion
  20.7 0.9 copy-done
  21.6 1.2 reverse_bitcast_fusion.1
  22.8 0.0 all-reduce.10.cloned.1.call-update
  22.8 0.0 copy-done.5
  22.8 0.1 copy.59
  23.0 0.5 collective-permute-start
  23.5 1.3 constant_dynamic-slice_fusion
  24.7 0.2 copy.58
  25.0 0.0 collective-permute-done
  25.0 52.5 %all-reduce.10.cloned.1.call-done = bf16[2,64,16,16,8]{1,3,2,4,0:T(8,128)(2,1)} async-done(((bf16[2,64,16,16,8]{1,3,2,4,0:T(8,128)(2,1)}), bf16[2,64,16,16,8]{1,3,2,4,0:T(8,128)(2,1)}) %all-reduce.10.cloned.1.call-update) | async-done | bytes 524304 | tf_op jit(solution)/shard_map/psum | solution.py:161
  77.5 1.1 slice.86
  78.6 0.3 copy.24
  78.9 0.2 copy.27.w_ref
  79.1 9.3 %shard_map.76 = (bf16[32,64,128]{2,1,0:T(8,128)(2,1)S(1)}, bf16[32,64,128]{2,1,0:T(8,128)(2,1)S(1)}) custom-call(f32[48,8,128]{2,1,0:T(8,128)S(1)} %maximum_convert_fusion.x_ref, bf16[64,2048]{1,0:T(8,128)(2,1)S(1)} %copy.27.w_ref, bf16[32,64,128]{2,1,0:T(8,128)(2,1)S(1)} %bitcast.107), custom_call_target="tpu_custom_call" | custom-call | flops 1073741824 | bytes 2097152 | tf_op jit(solution)/shard_map/pallas_call | solution.py:31
  88.5 0.1 collective-permute-start.1
  89.9 0.2 collective-permute-done.1
  90.2 5.1 %shard_map.77 = bf16[32,8,128]{2,1,0:T(8,128)(2,1)S(1)} custom-call(bf16[64,2048]{1,0:T(8,128)(2,1)S(1)} %copy.27.w_ref, bf16[512,128]{1,0:T(8,128)(2,1)S(1)} %bitcast.115, bf16[2048,128]{1,0:T(8,128)(2,1)S(1)} %bitcast.104, bf16[512,128]{1,0:T(8,128)(2,1)S(1)} %bitcast.114), custom_call_target="tpu_custom_call" | custom-call | flops 1073741824 | bytes 2097152 | tf_op jit(solution)/shard_map/pallas_call | solution.py:31
  95.3 1.5 collective-permute-start.2
  96.8 0.2 bitcast_select_fusion.prev_ref
  97.0 2.6 %collective-permute-done.2 = bf16[32,8,128]{2,1,0:T(8,128)(2,1)S(1)} collective-permute-done((bf16[32,8,128]{2,1,0:T(8,128)(2,1)S(1)}, bf16[32,8,128]{2,1,0:T(8,128)(2,1)S(1)}, u32[]{:S(2)}, u32[]{:S(2)}) %collective-permute-start.2) | collective-permute-done | bytes 65568 | tf_op jit(solution)/shard_map/ppermute | solution.py:215
  99.6 0.1 fusion.13
  99.7 0.0 copy-start.3
  99.7 0.0 copy-start.4
  99.8 0.1 collective-permute-start.3
  99.8 6.8 %shard_map.78 = f32[64,2048]{1,0:T(8,128)} custom-call(f32[32,8,128]{2,1,0:T(8,128)S(1)} %get-tuple-element.46.x_ref, bf16[512,128]{1,0:T(8,128)(2,1)S(1)} %bitcast.113, bf16[2048,128]{1,0:T(8,128)(2,1)S(1)} %bitcast.98, bf16[512,128]{1,0:T(8,128)(2,1)S(1)} %bitcast.112), custom_call_target="tpu_custom_call" | custom-call | flops 1073741824 | bytes 2097152 | tf_op jit(solution)/shard_map/pallas_call | solution.py:31
  106.7 0.0 copy-done.3
  106.7 1.5 conditional.1
  106.7 1.2 copy.46
  108.0 0.2 copy.44
  108.2 0.2 all-reduce.12.cloned.1.call-start
  108.4 0.0 collective-permute-done.3
  108.5 9.3 %shard_map.79 = (bf16[32,64,128]{2,1,0:T(8,128)(2,1)S(1)}, bf16[32,64,128]{2,1,0:T(8,128)(2,1)S(1)}) custom-call(f32[48,8,128]{2,1,0:T(8,128)S(1)} %maximum_convert_fusion.1.x_ref, bf16[64,2048]{1,0:T(8,128)(2,1)S(1)} %get-tuple-element.42.w_ref, bf16[32,64,128]{2,1,0:T(8,128)(2,1)S(1)} %bitcast_select_fusion.prev_ref), custom_call_target="tpu_custom_call" | custom-call | flops 1073741824 | bytes 2097152 | tf_op jit(solution)/shard_map/pallas_call | solution.py:31
  117.8 0.6 collective-permute-start.4
  118.3 1.2 collective-permute-done.4
  119.6 5.1 %shard_map.80 = bf16[32,8,128]{2,1,0:T(8,128)(2,1)S(1)} custom-call(bf16[64,2048]{1,0:T(8,128)(2,1)S(1)} %get-tuple-element.42.w_ref, bf16[512,128]{1,0:T(8,128)(2,1)S(1)} %bitcast.110, bf16[2048,128]{1,0:T(8,128)(2,1)S(1)} %bitcast.106, bf16[512,128]{1,0:T(8,128)(2,1)S(1)} %bitcast.111), custom_call_target="tpu_custom_call" | custom-call | flops 1073741824 | bytes 2097152 | tf_op jit(solution)/shard_map/pallas_call | solution.py:31
  124.7 1.5 collective-permute-start.5
  126.3 2.9 %collective-permute-done.5 = bf16[32,8,128]{2,1,0:T(8,128)(2,1)S(1)} collective-permute-done((bf16[32,8,128]{2,1,0:T(8,128)(2,1)S(1)}, bf16[32,8,128]{2,1,0:T(8,128)(2,1)S(1)}, u32[]{:S(2)}, u32[]{:S(2)}) %collective-permute-start.5) | collective-permute-done | bytes 65568 | tf_op jit(solution)/shard_map/ppermute | solution.py:215
  129.1 0.1 convert_convert_fusion
  129.2 6.8 %shard_map.81 = f32[64,2048]{1,0:T(8,128)} custom-call(f32[32,8,128]{2,1,0:T(8,128)S(1)} %get-tuple-element.52.x_ref, bf16[512,128]{1,0:T(8,128)(2,1)S(1)} %bitcast.108, bf16[2048,128]{1,0:T(8,128)(2,1)S(1)} %bitcast.101, bf16[512,128]{1,0:T(8,128)(2,1)S(1)} %bitcast.109), custom_call_target="tpu_custom_call" | custom-call | flops 1073741824 | bytes 2097152 | tf_op jit(solution)/shard_map/pallas_call | solution.py:31
  136.1 0.0 all-reduce.12.cloned.1.call-update
  136.1 0.1 maximum_bitcast_fusion
  136.2 1.6 copy.42
  137.9 0.7 copy.41
  138.5 56.1 %all-reduce.12.cloned.1.call-done = (f32[64,2048]{1,0:T(8,128)}, f32[64,2048]{1,0:T(8,128)}) async-done(((f32[64,2048]{1,0:T(8,128)}, f32[64,2048]{1,0:T(8,128)}), (f32[64,2048]{1,0:T(8,128)}, f32[64,2048]{1,0:T(8,128)})) %all-reduce.12.cloned.1.call-update) | async-done | bytes 1048592 | tf_op jit(solution)/shard_map/psum | solution.py:174
  194.7 1.1 broadcast_multiply_fusion.2
  195.8 0.0 copy-start.1
  195.8 1.3 copy.34
  197.1 1.5 copy.35
  198.6 0.3 fusion.6
  198.9 0.0 copy-done.6
  198.9 0.9 broadcast_multiply_fusion.1
  199.8 2.4 %copy.38 = f32[64,2048]{0,1:T(8,128)} copy(f32[64,2048]{1,0:T(8,128)} %broadcast_multiply_fusion.1) | data formatting | bytes 1048576 | tf_op jit(solution)/shard_map/div | solution.py:167
  202.1 1.4 copy.39
  203.5 0.2 select_dynamic-update-slice_fusion.2
  203.7 0.3 fusion.4
  204.0 0.2 select_dynamic-update-slice_fusion.1
  204.2 1.6 copy.43
  (20 shorter events, 0.4 us)
Async XLA Ops:
  7.2 70.3 %all-reduce.10.cloned.1.call-start = ((), (), s32[]{:S(2)}) async-start(), calls=%async_computation.2 | async-start | bytes 2097152 | tf_op jit(solution)/shard_map/psum | solution.py:161
  20.3 1.3 copy-start
  21.6 1.2 copy-start.5
  23.0 2.0 collective-permute-start
  88.5 1.6 collective-permute-start.1
  95.3 4.4 %collective-permute-start.2 = (bf16[32,8,128]{2,1,0:T(8,128)(2,1)S(1)}, bf16[32,8,128]{2,1,0:T(8,128)(2,1)S(1)}, u32[]{:S(2)}, u32[]{:S(2)}) collective-permute-start(bf16[32,8,128]{2,1,0:T(8,128)(2,1)S(1)} %shard_map.77), channel_id=1, source_target_pairs={{0,2},{2,0},{1,3},{3,1},{4,6},{6,4},{5,7},{7,5},{8,10},{10,8},{9,1... | collective-permute-start | bytes 196616 | tf_op jit(solution)/shard_map/ppermute | solution.py:215
  99.7 7.0 %copy-start.3 = (f32[2,64,2048]{2,1,0:T(8,128)S(1)}, f32[2,64,2048]{2,1,0:T(8,128)}, u32[]{:S(2)}) copy-start(f32[2,64,2048]{2,1,0:T(8,128)} %param.9) | copy-start | bytes 3145732
  99.7 7.0 %copy-start.4 = (bf16[2,64,16,16,8]{1,3,2,4,0:T(8,128)(2,1)S(1)}, bf16[2,64,16,16,8]{1,3,2,4,0:T(8,128)(2,1)}, u32[]{:S(2)}) copy-start(bf16[2,64,16,16,8]{1,3,2,4,0:T(8,128)(2,1)} %all-reduce.10.cloned.1.call-done) | copy-start | bytes 1572868
  99.8 8.6 %collective-permute-start.3 = (bf16[8,8,128]{2,1,0:T(8,128)(2,1)S(1)}, bf16[8,8,128]{2,1,0:T(8,128)(2,1)S(1)}, u32[]{:S(2)}, u32[]{:S(2)}) collective-permute-start(bf16[8,8,128]{2,1,0:T(8,128)(2,1)S(1)} %slice_select_fusion), channel_id=1, source_target_pairs={{0,1},{1,0},{2,3},{3,2},{4,5},{5,4},{6,7},{7,6},{8,9},{9,8},{10,11... | collective-permute-start | bytes 49160 | tf_op jit(solution)/shard_map/ppermute | solution.py:139
  108.2 86.5 %all-reduce.12.cloned.1.call-start = ((), (), s32[]{:S(2)}) async-start(), calls=%async_computation.3 | async-start | bytes 2097152 | tf_op jit(solution)/shard_map/psum | solution.py:174
  117.8 1.7 collective-permute-start.4
  124.7 4.4 %collective-permute-start.5 = (bf16[32,8,128]{2,1,0:T(8,128)(2,1)S(1)}, bf16[32,8,128]{2,1,0:T(8,128)(2,1)S(1)}, u32[]{:S(2)}, u32[]{:S(2)}) collective-permute-start(bf16[32,8,128]{2,1,0:T(8,128)(2,1)S(1)} %shard_map.80), channel_id=1, source_target_pairs={{0,2},{2,0},{1,3},{3,1},{4,6},{6,4},{5,7},{7,5},{8,10},{10,8},{9,1... | collective-permute-start | bytes 196616 | tf_op jit(solution)/shard_map/ppermute | solution.py:215
  195.8 2.8 %copy-start.1 = (f32[2,64,2048]{1,2,0:T(8,128)S(1)}, f32[2,64,2048]{1,2,0:T(8,128)}, u32[]{:S(2)}) copy-start(f32[2,64,2048]{1,2,0:T(8,128)} %copy-done) | copy-start | bytes 3145732
  197.1 1.8 copy-start.6
Sparse Core Ops, SparseCore 0:
  23.0 54.5 all-reduce.9
  136.2 58.4 all-reduce.11

commit v2 on v1

--- a/solution.py
+++ b/solution.py
@@ -25,6 +25,7 @@
 BF16 = jnp.bfloat16
 F32 = jnp.float32
 VMEM_LIMIT = 40 * 1024 * 1024
+MESH = pl.DeviceIdType.MESH
 
 
 def call(body, out_shape, scratch, flops, args):
@@ -134,6 +135,96 @@
         out_ref[:, p * QC : (p + 1) * QC] = total[p * count : (p + 1) * count, :]
 
 
+def tile_sum_body(count, paired, x_ref, out_ref, *scratch):
+    got, mine, send_sems, recv_sems = scratch[:4]
+    me = lax.axis_index("tile")
+    half = lax.axis_index("sub")
+    peers = [lax.rem(me + d, count) for d in range(1, count)]
+    barrier = pltpu.get_barrier_semaphore()
+    for peer in peers:
+        pl.semaphore_signal(barrier, inc=1, device_id={"tile": peer}, device_id_type=MESH)
+    pl.semaphore_signal(barrier, inc=1, device_id={"sub": 1 - half}, device_id_type=MESH)
+    pl.semaphore_wait(barrier, count)
+
+    def remote(src, dst, at, where):
+        return pltpu.make_async_remote_copy(
+            src_ref=src,
+            dst_ref=dst,
+            send_sem=send_sems.at[at],
+            recv_sem=recv_sems.at[at],
+            device_id=where,
+            device_id_type=MESH,
+        )
+
+    if paired:
+        other = scratch[4]
+        cross = remote(x_ref.at[1 - half], other, 3 * count, {"sub": 1 - half})
+        cross.start()
+        cross.wait()
+        for part in range(count):
+            mine[part] = (x_ref[half, part] + other[part]).astype(BF16)
+    scattered = []
+    for d, peer in enumerate(peers):
+        source = mine.at[peer] if paired else x_ref.at[half, peer]
+        copy = remote(source, got.at[d], d, {"tile": peer})
+        copy.start()
+        scattered.append(copy)
+    if paired:
+        total = x_ref[half, me] + other[me]
+    else:
+        total = x_ref[half, me].astype(F32)
+    for d, copy in enumerate(scattered):
+        copy.wait_recv()
+        total = total + got[d].astype(F32)
+    out_ref[half, me] = total.astype(BF16)
+    gathered, crossed = [], []
+    for d, peer in enumerate(peers):
+        copy = remote(out_ref.at[half, me], out_ref.at[half, me], count + d, {"tile": peer})
+        copy.start()
+        gathered.append(copy)
+
+    def forward(at, part):
+        copy = remote(out_ref.at[half, part], out_ref.at[half, part], at, {"sub": 1 - half})
+        copy.start()
+        crossed.append(copy)
+
+    forward(2 * count, me)
+    for d, copy in enumerate(gathered):
+        copy.wait_recv()
+        forward(2 * count + 1 + d, lax.rem(me + count - 1 - d, count))
+    for copy in scattered + gathered:
+        copy.wait_send()
+    for copy in crossed:
+        copy.wait()
+
+
+def tile_sum(x, paired, ident):
+    count = lax.axis_size("tile")
+    wide = x.size // (2 * count * 16)
+    if wide < COLS or lax.axis_size("sub") != 2:
+        return lax.psum(x, ("tile", "sub") if paired else "tile")
+    block = (count, 16, wide)
+    scratch = [
+        pltpu.VMEM((count - 1, 16, wide), BF16),
+        pltpu.VMEM(block, BF16),
+        pltpu.SemaphoreType.DMA((3 * count + 1,)),
+        pltpu.SemaphoreType.DMA((3 * count + 1,)),
+    ]
+    if paired:
+        scratch.append(pltpu.VMEM(block, F32))
+    out = pl.pallas_call(
+        functools.partial(tile_sum_body, count, paired),
+        out_shape=jax.ShapeDtypeStruct((2,) + block, BF16),
+        in_specs=[pl.BlockSpec(memory_space=pltpu.VMEM)],
+        out_specs=pl.BlockSpec(memory_space=pltpu.VMEM),
+        scratch_shapes=scratch,
+        compiler_params=pltpu.CompilerParams(
+            collective_id=ident, has_side_effects=True, vmem_limit_bytes=VMEM_LIMIT
+        ),
+    )(x.reshape((2,) + block))
+    return out.reshape(x.shape)
+
+
 def swap_halo(x, place):
     send = jnp.where(place == 0, x[ROWS - HALO :], x[:HALO])
     got = lax.ppermute(send, "sub", [(0, 1), (1, 0)])
@@ -153,12 +244,12 @@
     def picked(store, s):
         return lax.dynamic_index_in_dim(store, holders[s] % slot_count, 0, keepdims=False)
 
-    def shared(stores):
+    def shared(stores, ident):
         sent = [
             jnp.where(tile_place == holders[s] // slot_count, picked(store, s).astype(BF16), jnp.zeros((), BF16))
             for s, store in stores
         ]
-        whole = lax.psum(jnp.stack(sent), "tile")
+        whole = tile_sum(jnp.stack(sent), False, ident)
         cut = whole.reshape(-1, count, C, PATCH, PATCH)[:, :, :, ::-1]
         return cut.transpose(0, 1, 3, 4, 2).reshape(-1, count, FEAT)
 
@@ -170,14 +261,14 @@
         written = lax.dynamic_update_index_in_dim(store, final, holders[s] % slot_count, 0)
         return jnp.where(tile_place == holders[s] // slot_count, written, store)
 
-    def summed(local):
-        whole = lax.psum(local, ("tile", "sub"))
-        return whole.reshape(count, PATCH, PATCH, C).transpose(0, 3, 1, 2).reshape(count, FEAT)
+    def summed(local, ident):
+        whole = tile_sum(jnp.stack(local), True, ident).astype(F32)
+        return whole.reshape(-1, count, PATCH, PATCH, C).transpose(0, 1, 4, 2, 3).reshape(-1, count, FEAT)
 
     current = residual[0].transpose(1, 0, 2)
-    first_pair = shared([(0, filter_store), (1, filter_store)])
+    first_pair = shared([(0, filter_store), (1, filter_store)], 0)
     weights = first_pair[0]
-    fresh_maps, local_grads, sums = [], [], []
+    fresh_maps, local_grads = [], []
     same = plan[0] == plan[1]
     for s in range(STEPS):
         previous = lax.dynamic_index_in_dim(coefficients[0], plan[s], 0, keepdims=False).transpose(1, 0, 2)
@@ -185,7 +276,7 @@
             previous = jnp.where(same, fresh_maps[0], previous)
             weights = lax.cond(
                 same,
-                lambda local, pair: shared([(1, updated(filter_store, 0, summed(local)))])[0],
+                lambda local, pair: shared([(1, updated(filter_store, 0, summed([local], 2)[0]))], 3)[0],
                 lambda local, pair: pair[1],
                 local_grads[0],
                 first_pair,
@@ -227,7 +318,7 @@
         )
         fresh_maps.append(fresh)
         local_grads.append(local)
-        sums.append(summed(local))
+    sums = summed(local_grads, 1)
     store = filter_store
     for s in range(STEPS):
         store = updated(store, s, sums[s])

time: 213 us -> 158 us (0.74)
  waiting for transfers between devices: 116 us -> 4.87 us
  Pallas kernels: 42.4 us -> 79 us
  local copies, waits for them, and re-layouts: 21.7 us -> 54.9 us
  between operations: 24.3 us -> 11 us
    psum x2 -> x0, waiting for transfers between devices: 109 us -> none  [the longest x1 56.1 us: summed(): whole = lax.psum(local, ('tile', 'sub'))]
    pallas_call x0 -> x2, Pallas kernels: none -> 38.2 us  [tile_sum(): pl.pallas_call(functools.partial(tile_sum_body, count, paired), out_shape...]
    transpose x0 -> x2, local copies, waits for them, and re-layouts: none -> 11.8 us  [summed(): whole.reshape(-1, count, PATCH, PATCH, C).transpose(0, 1, 4, 2, 3)]
    rev x0 -> x1, local copies, waits for them, and re-layouts: none -> 10.6 us  [shared(): cut = whole.reshape(-1, count, C, PATCH, PATCH)[:, :, :, ::-1]]
    div x4 -> x2, local copies, waits for them, and re-layouts: 6.57 us -> 0.41 us  [updated(): moved = master - FILTER_STEP * grads / pixel_total]
    transpose x1, local copies, waits for them, and re-layouts: 1.16 us -> 6.47 us  [shared(): return cut.transpose(0, 1, 3, 4, 2).reshape(-1, count, FEAT)]
    another operation x0 -> x1, local copies, waits for them, and re-layouts: none -> 4.5 us  [shared(): cut = whole.reshape(-1, count, C, PATCH, PATCH)[:, :, :, ::-1]]
    slice x2, local copies, waits for them, and re-layouts: 1.42 us -> 4.48 us  [per_device(): weights = first_pair[0]]
  transfers between devices with their start and end apart: 8 -> 6, of which waited for: 6 -> 3; matrix products, arithmetic and copies ran while one was open for 3% -> 23% of each run, Pallas kernels for 3% -> 16%
where the time goes in v2:
time: 158 us; the launch traced here: 157 us
  Pallas kernels  79 us (50%)
  local copies, waits for them, and re-layouts  54.9 us (35%)
  between operations  11 us (7%)
  waiting for transfers between devices  4.87 us (3%)
  starting transfers between devices  4.7 us (3%)
  other arithmetic  2.23 us (1%)
    pallas_call x6, Pallas kernels, call(): pl.pallas_call(body, out_shape=out_shape, in_specs=[pl.BlockSpec(memory_s...  40.8 us
    pallas_call x2, Pallas kernels, tile_sum(): pl.pallas_call(functools.partial(tile_sum_body, count, paired), out_shape...  38.2 us
    transpose x2, local copies, waits for them, and re-layouts, summed(): whole.reshape(-1, count, PATCH, PATCH, C).transpose(0, 1, 4, 2, 3)  11.8 us
    rev x1, local copies, waits for them, and re-layouts, shared(): cut = whole.reshape(-1, count, C, PATCH, PATCH)[:, :, :, ::-1]  10.6 us
    unnamed x15, local copies, waits for them, and re-layouts  9.69 us
    transpose x1, local copies, waits for them, and re-layouts, shared(): return cut.transpose(0, 1, 3, 4, 2).reshape(-1, count, FEAT)  6.47 us
    another operation x1, local copies, waits for them, and re-layouts, shared(): cut = whole.reshape(-1, count, C, PATCH, PATCH)[:, :, :, ::-1]  4.5 us
    slice x2, local copies, waits for them, and re-layouts, per_device(): weights = first_pair[0]  4.48 us
  transfers between devices with their start and end apart: 6, of which 3 were waited for; matrix products, arithmetic and copies ran while one was open for 23% of the time, Pallas kernels for 16%

profile of v2, /device:TPU:0, one launch (start us, length us, event | category | flops | bytes accessed | tf_op | source)
XLA Modules:
  0.0 157.0 jit_solution(16433820689544835739)
XLA Ops:
  0.6 1.0 copy.60
  1.6 0.5 collective-permute-start
  2.2 1.3 fusion.26
  7.4 1.3 fusion.25
  13.4 1.8 %copy.23 = f32[2,64,2048]{1,2,0:T(8,128)S(1)} copy(f32[2,64,2048]{2,1,0:T(8,128)} %param.9) | data formatting | bytes 2097152 | tf_op args[2]
  15.3 0.0 copy-start
  15.3 0.1 fusion.13
  15.4 0.2 copy.24
  15.6 0.2 copy.26
  15.8 0.8 copy-done
  16.6 0.1 pad_maximum_fusion.1.x_ref
  16.7 2.1 %constant_dynamic-slice_fusion = (bf16[1,1,64,32,128]{4,3,2,1,0:T(8,128)(2,1)S(1)}, bf16[1,1,64,32,128]{4,3,2,1,0:T(8,128)(2,1)}) fusion(bf16[1,8,64,32,128]{4,3,2,1,0:T(8,128)(2,1)} %param.8, s32[]{:T(128)S(6)} %select_n.194, s32[]{:T(128)S(6)} %select_n.188), kind=kLoop, calls=%fused_computation.57 | loop fusion | bytes 2097160 | tf_op jit(solution)/shard_map/jit(dynamic_index_in_dim)/dynamic_slice | solution.py:274
  18.7 18.6 %shard_map.76 = bf16[2,4,16,2048]{3,2,1,0:T(8,128)(2,1)S(1)} custom-call(bf16[2,4,16,2048]{3,2,1,0:T(8,128)(2,1)S(1)} %pad_maximum_fusion.1.x_ref), custom_call_target="tpu_custom_call" | custom-call | tf_op jit(solution)/shard_map/pallas_call | solution.py:215
  37.3 4.5 %reshape_reshape.3 = bf16[2,64,8,16,16]{4,3,2,1,0:T(8,128)(2,1)} reshape(bf16[2,4,16,2048]{3,2,1,0:T(8,128)(2,1)S(1)} %shard_map.76) | data formatting | bytes 1048576 | tf_op jit(solution)/shard_map/reshape;reshape | solution.py:253
  41.8 10.6 %rev.6 = bf16[2,64,8,16,16]{4,3,2,1,0:T(8,128)(2,1)} reverse(bf16[2,64,8,16,16]{4,3,2,1,0:T(8,128)(2,1)} %reshape_reshape.3), dimensions={3} | reverse | bytes 1048576 | tf_op jit(solution)/shard_map/rev | solution.py:253
  52.4 2.0 %slice.96 = bf16[1,64,16,16,8]{3,2,4,1,0:T(8,128)(2,1)S(1)} slice(bf16[2,64,16,16,8]{3,2,4,1,0:T(8,128)(2,1)} %bitcast.134), slice={[0:1], [0:64], [0:16], [0:16], [0:8]} | slice | bytes 524288 | tf_op jit(solution)/shard_map/slice | solution.py:270
  54.4 2.5 %copy.27 = bf16[1,64,16,16,8]{1,4,3,2,0:T(8,128)(2,1)S(1)} copy(bf16[1,64,16,16,8]{3,2,4,1,0:T(8,128)(2,1)S(1)} %slice.96) | data formatting | bytes 524288 | tf_op jit(solution)/shard_map/slice | solution.py:270
  56.9 0.2 copy.30.w_ref
  57.1 1.2 copy.59
  58.4 0.0 collective-permute-done
  58.4 9.3 %shard_map.77 = (bf16[32,64,128]{2,1,0:T(8,128)(2,1)S(1)}, bf16[32,64,128]{2,1,0:T(8,128)(2,1)S(1)}) custom-call(f32[48,8,128]{2,1,0:T(8,128)S(1)} %maximum_convert_fusion.x_ref, bf16[64,2048]{1,0:T(8,128)(2,1)S(1)} %copy.30.w_ref, bf16[32,64,128]{2,1,0:T(8,128)(2,1)S(1)} %bitcast.123), custom_call_target="tpu_custom_call" | custom-call | flops 1073741824 | bytes 2097152 | tf_op jit(solution)/shard_map/pallas_call | solution.py:32
  67.7 0.4 collective-permute-start.1
  69.5 0.0 collective-permute-done.1
  69.6 0.0 copy-start.4
  69.6 5.1 %shard_map.78 = bf16[32,8,128]{2,1,0:T(8,128)(2,1)S(1)} custom-call(bf16[64,2048]{1,0:T(8,128)(2,1)S(1)} %copy.30.w_ref, bf16[512,128]{1,0:T(8,128)(2,1)S(1)} %bitcast.132, bf16[2048,128]{1,0:T(8,128)(2,1)S(1)} %bitcast.120, bf16[512,128]{1,0:T(8,128)(2,1)S(1)} %bitcast.131), custom_call_target="tpu_custom_call" | custom-call | flops 1073741824 | bytes 2097152 | tf_op jit(solution)/shard_map/pallas_call | solution.py:32
  74.7 1.6 collective-permute-start.2
  76.3 0.2 bitcast_select_fusion.prev_ref
  76.5 2.6 %collective-permute-done.2 = bf16[32,8,128]{2,1,0:T(8,128)(2,1)S(1)} collective-permute-done((bf16[32,8,128]{2,1,0:T(8,128)(2,1)S(1)}, bf16[32,8,128]{2,1,0:T(8,128)(2,1)S(1)}, u32[]{:S(2)}, u32[]{:S(2)}) %collective-permute-start.2) | collective-permute-done | bytes 65568 | tf_op jit(solution)/shard_map/ppermute | solution.py:306
  79.0 0.0 copy-done.4
  79.0 0.1 fusion.19
  79.2 0.1 collective-permute-start.3
  79.2 6.0 %shard_map.79 = f32[64,2048]{1,0:T(8,128)S(1)} custom-call(f32[32,8,128]{2,1,0:T(8,128)S(1)} %get-tuple-element.44.x_ref, bf16[512,128]{1,0:T(8,128)(2,1)S(1)} %bitcast.130, bf16[2048,128]{1,0:T(8,128)(2,1)S(1)} %bitcast.114, bf16[512,128]{1,0:T(8,128)(2,1)S(1)} %bitcast.129), custom_call_target="tpu_custom_call" | custom-call | flops 1073741824 | bytes 2097152 | tf_op jit(solution)/shard_map/pallas_call | solution.py:32
  85.3 0.0 copy-start.2
  85.3 0.8 copy-done.2
  86.1 7.1 %conditional.1 = (bf16[64,2048]{1,0:T(8,128)(2,1)S(1)}) conditional(s32[]{:T(128)} %convert_element_type.74, (bf16[2,64,16,16,8]{3,2,4,1,0:T(8,128)(2,1)}) %tuple.41, (s32[]{:T(128)}, s32[]{:T(128)}, s32[]{:T(128)}, f32[2,64,2048]{2,1,0:T(8,128)}, f32[64,2048]{1,0:T(8,128)S(1)}) %tuple.14), branch_computations={%region_0.1_spmd, %region_1.3_spmd} | conditional | flops 1179758 | bytes 13371106 | solution.py:277
  86.1 6.5 %copy.47 = bf16[2,64,16,16,8]{1,4,3,2,0:T(8,128)(2,1)S(1)} copy(bf16[2,64,16,16,8]{3,2,4,1,0:T(8,128)(2,1)} %get-tuple-element.43) | data formatting | bytes 1048576 | tf_op jit(solution)/shard_map/transpose | solution.py:254
  92.6 0.2 copy.45
  93.2 0.0 collective-permute-done.3
  93.3 9.3 %shard_map.80 = (bf16[32,64,128]{2,1,0:T(8,128)(2,1)S(1)}, bf16[32,64,128]{2,1,0:T(8,128)(2,1)S(1)}) custom-call(f32[48,8,128]{2,1,0:T(8,128)S(1)} %maximum_convert_fusion.1.x_ref, bf16[64,2048]{1,0:T(8,128)(2,1)S(1)} %get-tuple-element.42.w_ref, bf16[32,64,128]{2,1,0:T(8,128)(2,1)S(1)} %bitcast_select_fusion.prev_ref), custom_call_target="tpu_custom_call" | custom-call | flops 1073741824 | bytes 2097152 | tf_op jit(solution)/shard_map/pallas_call | solution.py:32
  102.6 0.6 collective-permute-start.4
  103.2 1.2 collective-permute-done.4
  104.4 5.1 %shard_map.81 = bf16[32,8,128]{2,1,0:T(8,128)(2,1)S(1)} custom-call(bf16[64,2048]{1,0:T(8,128)(2,1)S(1)} %get-tuple-element.42.w_ref, bf16[512,128]{1,0:T(8,128)(2,1)S(1)} %bitcast.127, bf16[2048,128]{1,0:T(8,128)(2,1)S(1)} %bitcast.122, bf16[512,128]{1,0:T(8,128)(2,1)S(1)} %bitcast.128), custom_call_target="tpu_custom_call" | custom-call | flops 1073741824 | bytes 2097152 | tf_op jit(solution)/shard_map/pallas_call | solution.py:32
  109.5 1.6 %collective-permute-start.5 = (bf16[32,8,128]{2,1,0:T(8,128)(2,1)S(1)}, bf16[32,8,128]{2,1,0:T(8,128)(2,1)S(1)}, u32[]{:S(2)}, u32[]{:S(2)}) collective-permute-start(bf16[32,8,128]{2,1,0:T(8,128)(2,1)S(1)} %shard_map.81), channel_id=1, source_target_pairs={{0,2},{2,0},{1,3},{3,1},{4,6},{6,4},{5,7},{7,5},{8,10},{10,8},{9,1... | collective-permute-start | bytes 196616 | tf_op jit(solution)/shard_map/ppermute | solution.py:306
  111.1 0.1 maximum_bitcast_fusion
  111.2 1.6 %copy.43 = bf16[1,2,64,32,128]{4,3,2,1,0:T(8,128)(2,1)} copy(bf16[1,2,64,32,128]{4,2,3,1,0:T(8,128)(2,1)S(1)} %maximum_bitcast_fusion) | data formatting | bytes 2097152
  112.9 1.1 collective-permute-done.5
  114.0 0.1 convert_convert_fusion
  114.1 0.0 copy-start.3
  114.1 6.0 %shard_map.82 = f32[64,2048]{1,0:T(8,128)S(1)} custom-call(f32[32,8,128]{2,1,0:T(8,128)S(1)} %get-tuple-element.52.x_ref, bf16[512,128]{1,0:T(8,128)(2,1)S(1)} %bitcast.125, bf16[2048,128]{1,0:T(8,128)(2,1)S(1)} %bitcast.118, bf16[512,128]{1,0:T(8,128)(2,1)S(1)} %bitcast.126), custom_call_target="tpu_custom_call" | custom-call | flops 1073741824 | bytes 2097152 | tf_op jit(solution)/shard_map/pallas_call | solution.py:32
  120.1 0.0 copy-done.3
  120.1 0.1 pad_maximum_fusion.x_ref
  120.2 19.6 %shard_map.83 = bf16[2,4,16,2048]{3,2,1,0:T(8,128)(2,1)S(1)} custom-call(f32[2,4,16,2048]{3,2,1,0:T(8,128)S(1)} %pad_maximum_fusion.x_ref), custom_call_target="tpu_custom_call" | custom-call | tf_op jit(solution)/shard_map/pallas_call | solution.py:215
  139.8 5.3 %copy.36 = f32[2,4,16,2048]{2,1,3,0:T(4,128)} copy(bf16[2,4,16,2048]{3,2,1,0:T(8,128)(2,1)S(1)} %shard_map.83) | data formatting | bytes 1572864 | tf_op jit(solution)/shard_map/transpose | solution.py:266
  145.2 6.5 %reshape.171 = f32[2,64,16,16,8]{1,4,3,2,0:T(8,128)S(1)} reshape(f32[2,4,16,2048]{2,1,3,0:T(4,128)} %copy.36) | data formatting | bytes 2097152 | tf_op jit(solution)/shard_map/transpose | solution.py:266
  151.7 0.2 slice_multiply_fusion
  151.9 0.2 copy.37
  152.1 1.4 copy-done.1
  153.5 0.3 fusion.10
  153.8 0.2 constant_dynamic-update-slice_fusion.2
  154.0 0.2 copy.40
  154.2 0.3 fusion.6
  154.5 0.2 constant_dynamic-update-slice_fusion.1
  154.8 1.6 copy.44
  156.3 0.7 copy.42
  (17 shorter events, 0.4 us)
Async XLA Ops:
  1.6 56.7 %collective-permute-start = (bf16[8,8,128]{2,1,0:T(8,128)(2,1)S(1)}, bf16[8,8,128]{2,1,0:T(8,128)(2,1)S(1)}, u32[]{:S(2)}, u32[]{:S(2)}) collective-permute-start(bf16[8,8,128]{2,1,0:T(8,128)(2,1)S(1)} %slice_select_fusion.1), channel_id=1, source_target_pairs={{0,1},{1,0},{2,3},{3,2},{4,5},{5,4},{6,7},{7,6},{8,9},{9,8},{10,11... | collective-permute-start | bytes 49160 | tf_op jit(solution)/shard_map/ppermute | solution.py:230
  15.3 1.3 copy-start
  67.7 1.7 %collective-permute-start.1 = (bf16[8,2,64,128]{3,2,0,1:T(8,128)(2,1)S(1)}, bf16[8,2,64,128]{3,2,0,1:T(8,128)(2,1)S(1)}, u32[]{:S(2)}, u32[]{:S(2)}) collective-permute-start(bf16[8,2,64,128]{3,2,0,1:T(8,128)(2,1)S(1)} %fusion.16), channel_id=1, source_target_pairs={{0,1},{1,0},{2,3},{3,2},{4,5},{5,4},{6,7},{7,6},{8,9},{9,8},{10,11... | collective-permute-start | bytes 786440 | tf_op jit(solution)/shard_map/ppermute | solution.py:230
  69.6 9.5 %copy-start.4 = (f32[1,8,32,128]{3,2,1,0:T(8,128)S(1)}, f32[1,8,32,128]{3,2,1,0:T(8,128)}, u32[]{:S(2)}) copy-start(f32[1,8,32,128]{3,2,1,0:T(8,128)} %param.7) | copy-start | bytes 393220
  74.7 4.3 %collective-permute-start.2 = (bf16[32,8,128]{2,1,0:T(8,128)(2,1)S(1)}, bf16[32,8,128]{2,1,0:T(8,128)(2,1)S(1)}, u32[]{:S(2)}, u32[]{:S(2)}) collective-permute-start(bf16[32,8,128]{2,1,0:T(8,128)(2,1)S(1)} %shard_map.78), channel_id=1, source_target_pairs={{0,2},{2,0},{1,3},{3,1},{4,6},{6,4},{5,7},{7,5},{8,10},{10,8},{9,1... | collective-permute-start | bytes 196616 | tf_op jit(solution)/shard_map/ppermute | solution.py:306
  79.2 14.1 %collective-permute-start.3 = (bf16[8,8,128]{2,1,0:T(8,128)(2,1)S(1)}, bf16[8,8,128]{2,1,0:T(8,128)(2,1)S(1)}, u32[]{:S(2)}, u32[]{:S(2)}) collective-permute-start(bf16[8,8,128]{2,1,0:T(8,128)(2,1)S(1)} %slice_select_fusion), channel_id=1, source_target_pairs={{0,1},{1,0},{2,3},{3,2},{4,5},{5,4},{6,7},{7,6},{8,9},{9,8},{10,11... | collective-permute-start | bytes 49160 | tf_op jit(solution)/shard_map/ppermute | solution.py:230
  85.3 0.8 copy-start.2
  102.6 1.7 %collective-permute-start.4 = (bf16[8,2,64,128]{3,2,0,1:T(8,128)(2,1)S(1)}, bf16[8,2,64,128]{3,2,0,1:T(8,128)(2,1)S(1)}, u32[]{:S(2)}, u32[]{:S(2)}) collective-permute-start(bf16[8,2,64,128]{3,2,0,1:T(8,128)(2,1)S(1)} %fusion.15), channel_id=1, source_target_pairs={{0,1},{1,0},{2,3},{3,2},{4,5},{5,4},{6,7},{7,6},{8,9},{9,8},{10,11... | collective-permute-start | bytes 786440 | tf_op jit(solution)/shard_map/ppermute | solution.py:230
  109.5 4.4 %collective-permute-start.5 = (bf16[32,8,128]{2,1,0:T(8,128)(2,1)S(1)}, bf16[32,8,128]{2,1,0:T(8,128)(2,1)S(1)}, u32[]{:S(2)}, u32[]{:S(2)}) collective-permute-start(bf16[32,8,128]{2,1,0:T(8,128)(2,1)S(1)} %shard_map.81), channel_id=1, source_target_pairs={{0,2},{2,0},{1,3},{3,1},{4,6},{6,4},{5,7},{7,5},{8,10},{10,8},{9,1... | collective-permute-start | bytes 196616 | tf_op jit(solution)/shard_map/ppermute | solution.py:306
  114.1 6.1 %copy-start.3 = (f32[64,2048]{1,0:T(8,128)S(1)}, f32[64,2048]{1,0:T(8,128)}, u32[]{:S(2)}) copy-start(f32[64,2048]{1,0:T(8,128)} %copy-done.2) | copy-start | bytes 1572868
  151.9 1.6 %copy-start.1 = (f32[2,64,2048]{1,2,0:T(8,128)S(1)}, f32[2,64,2048]{1,2,0:T(8,128)}, u32[]{:S(2)}) copy-start(f32[2,64,2048]{1,2,0:T(8,128)} %copy-done) | copy-start | bytes 3145732
